TPU v7x, 32 devices: a whole 2x2x4 slice. The times are simulated.
32 devices in a mesh: groups: 2 (over y), ctx: 4 (over z), peer: 4 (over x, core).
Axes of the slice: x: 2, y: 2, z: 4, core: 2. Of those that a mesh axis runs over, the one named last changes fastest.
Arguments:
- queries: bfloat16 [4, 4, 64, 128], P('groups'), parts along dimension 0, may hold values from -170 to 170
- key_cache: bfloat16 [4, 256, 8, 64, 128], P('groups', ('ctx', 'peer')), parts along dimension 0, may hold values from -6 to 6
- value_cache: bfloat16 [4, 256, 8, 64, 128], P('groups', ('ctx', 'peer')), parts along dimension 0, may hold values from -6 to 6
- page_list: int32 [4, 4, 8, 64], P('groups'), parts along dimension 0, may hold values from 0 to 255, as said below
- out_weight: bfloat16 [8192, 8192], P('ctx'), may hold values from -0.09375 to 0.09375
Outputs:
- layer_out: float32 [4, 4, 8192], P('groups', 'peer', 'ctx'), parts along dimension 0
There are 2 independent parts, one for each index of `groups`. A program takes and returns all parts, laid end to end along the dimension named above; an argument that names none is the same for every part. Nothing has to cross between parts.
Inputs may be any that keep to these rules, and one draw needn't show every extreme that they name: `page_list`: for each sequence, step and key head the 64 ids are distinct; each block of 16 consecutive pages holds at most 8 of them, and some block holds exactly 8.
All inputs are finite; a program needn't handle non-finite values.
Results may differ from a plain program's by a relative error of at most 0.005.
Values sent between devices are 32-bit elements; how exact they have to be, the bound alone decides.
A program may use at most 128 MiB of HBM per device.

v0:
```python
import jax
import jax.numpy as jnp
from jax import lax
from jax.sharding import PartitionSpec as P

masked_score = -1e30


def fold_over(outputs, maxima, totals):
    highest = jnp.max(maxima, axis=0)
    factor = jnp.exp(maxima - highest[None])
    new_totals = jnp.sum(factor * totals, axis=0)
    new_outputs = jnp.sum(factor[..., None] * outputs, axis=0)
    return (new_outputs, highest, new_totals)


def join_pair(former, latter):
    highest = jnp.maximum(former[1], latter[1])
    weight_b = jnp.exp(latter[1] - highest)
    outputs = latter[0] * weight_b[..., None]
    return (outputs, highest, latter[2] * weight_b)


def by_heads(array, ctx_size):
    dims = array.shape
    split_up = array.reshape(dims[:2] + (ctx_size, dims[2] // ctx_size) + dims[3:])
    return jnp.moveaxis(split_up, 2, 0)


def body(queries, key_cache, value_cache, page_list, out_weight):
    seq_count, step_count, head_count, head_width = queries.shape
    per_device = key_cache.shape[1]
    kv_heads = key_cache.shape[2]
    group_size = head_count // kv_heads
    ctx_size = lax.axis_size("ctx")
    peer_size = lax.axis_size("peer")
    ctx_index = lax.axis_index("ctx")
    peer_index = lax.axis_index("peer")
    head_share = head_count // ctx_size
    step_share = step_count // peer_size
    first_page = (ctx_index * peer_size + peer_index) * per_device
    local_ids = first_page + jnp.arange(per_device, dtype=jnp.int32)
    chosen = jnp.any(page_list[..., None] == local_ids, axis=3)
    grouped = queries.reshape(seq_count, step_count, kv_heads, group_size, head_width)
    scores = jnp.einsum(
        "bshgd,bphtd->bshgpt", grouped, key_cache, preferred_element_type=jnp.float32
    ) * head_width ** (-0.5)
    allowed = chosen[:, :, :, None, :, None]
    highest = jnp.max(jnp.where(allowed, scores, masked_score), axis=(4, 5))
    weights = jnp.where(allowed, jnp.exp(scores - highest[..., None, None]), 0.0)
    totals = jnp.sum(weights, axis=(4, 5))
    blended = jnp.einsum(
        "bshgpt,bphtd->bshgd",
        weights.astype(jnp.bfloat16),
        value_cache,
        preferred_element_type=jnp.float32,
    )
    blended = blended.reshape(seq_count, step_count, head_count, head_width)
    highest = highest.reshape(seq_count, step_count, head_count)
    totals = totals.reshape(seq_count, step_count, head_count)
    blocks = (
        by_heads(blended, ctx_size)[None],
        by_heads(highest, ctx_size)[None],
        by_heads(totals, ctx_size)[None],
    )
    start_state = (
        jnp.zeros((seq_count, step_count, head_share, head_width), jnp.float32),
        jnp.full((seq_count, step_count, head_share), masked_score, jnp.float32),
        jnp.zeros((seq_count, step_count, head_share), jnp.float32),
    )
    shards = (
        lax.all_gather(blocks[0], "ctx", axis=0, tiled=True),
        lax.all_gather(blocks[1], "ctx", axis=0, tiled=True),
        lax.all_gather(blocks[2], "ctx", axis=0, tiled=True),
    )
    own = tuple(
        (lax.dynamic_index_in_dim(member, ctx_index, 1, keepdims=False) for member in shards)
    )
    ctx_part = join_pair(start_state, fold_over(*own))
    arrived = (
        lax.all_to_all(ctx_part[0][None], "peer", split_axis=2, concat_axis=0, tiled=True),
        lax.all_to_all(ctx_part[1][None], "peer", split_axis=2, concat_axis=0, tiled=True),
        lax.all_to_all(ctx_part[2][None], "peer", split_axis=2, concat_axis=0, tiled=True),
    )
    combined = fold_over(*arrived)
    attended = (combined[0] / combined[2][..., None]).astype(jnp.bfloat16)
    attended = attended.reshape(seq_count * step_share, head_share * head_width)
    summed = lax.psum_scatter(
        lax.dot_general(
            out_weight, attended, (((0,), (1,)), ((), ())), preferred_element_type=jnp.float32
        ),
        "ctx",
        scatter_dimension=0,
        tiled=True,
    )
    return summed.T.reshape(seq_count, step_share, summed.shape[0])


def solution(mesh):
    in_specs = (
        P("groups", None, None, None),
        P("groups", ("ctx", "peer"), None, None, None),
        P("groups", ("ctx", "peer"), None, None, None),
        P("groups", None, None, None),
        P("ctx", None),
    )
    out_specs = P("groups", "peer", "ctx")
    return jax.shard_map(body, mesh=mesh, in_specs=in_specs, out_specs=out_specs, check_vma=False)
```

profile of v0, /device:TPU:0, one launch (start us, length us, event | category | flops | bytes accessed | tf_op | source)
XLA Modules:
  0.0 179.7 jit_solution(17065451049267508393)
XLA Ops:
  6.5 0.0 copy-start
  6.5 0.0 all-gather.5.cloned.1.call-start
  6.5 2.0 %compare_reduce_fusion = pred[2,4,8,16]{3,2,1,0:T(8,128)(4,1)S(1)} fusion(s32[2,4,8,64]{3,2,1,0:T(8,128)} %param.8, s32[16]{0:T(128)S(1)} %iota_add_fusion), kind=kLoop, calls=%fused_computation.18 | loop fusion | flops 130048 | bytes 17472 | tf_op jit(solution)/shard_map/reduce_or | solution.py:43
  8.6 0.2 copy.72
  8.8 0.0 copy-done
  8.8 0.0 copy-start.2
  8.8 6.1 %fusion.3 = (f32[2,4,8,8]{3,1,2,0:T(4,128)S(1)}, f32[2,8,16,64,4,8]{3,5,4,2,1,0:T(8,128)S(1)}) fusion(pred[2,4,8,16]{1,3,2,0:T(8,128)(4,1)S(1)} %copy.72, bf16[2,16,8,64,128]{4,3,2,1,0:T(8,128)(2,1)} %param.6, bf16[2,4,64,128]{3,2,1,0:T(8,128)(2,1)S(1)} %copy-done), kind=kOutput, calls=%fused_computation.6 | convolution fusion | flops 135790080 | bytes 6425600 | tf_op jit(solution)/shard_map/bshgd,bphtd->bshgpt/dot_general | solution.py:45
  14.9 0.0 copy-start.1
  14.9 0.0 copy-done.2
  14.9 5.0 %fusion.15 = f32[2,4,8,8,128]{4,3,1,2,0:T(8,128)S(1)} fusion(f32[2,8,16,64,4,8]{3,5,4,2,1,0:T(8,128)S(1)} %get-tuple-element.10, f32[2,4,8,8]{3,1,2,0:T(4,128)S(1)} %get-tuple-element.9, pred[2,4,8,16]{1,3,2,0:T(8,128)(4,1)S(1)} %copy.72, bf16[2,16,8,64,128]{4,3,2,1,0:T(8,128)(2,1)S(1)} %copy-done.2), kind=kOutput, calls=%fused_computation.17 | convolution fusion | flops 136314880 | bytes 6556672 | tf_op jit(solution)/shard_map/bshgpt,bphtd->bshgd/dot_general | solution.py:52
  19.9 0.0 copy-done.1
  19.9 0.7 copy.83
  20.6 0.0 all-gather.5.cloned.1.call-update
  20.7 0.1 reshape_reshape.9
  20.8 3.9 %fusion.8 = f32[2,4,8,8]{3,1,2,0:T(4,128)S(1)} fusion(f32[2,8,16,64,4,8]{3,5,4,2,1,0:T(8,128)} %copy-done.1, f32[2,4,8,8]{3,1,2,0:T(4,128)S(1)} %get-tuple-element.9, pred[2,4,8,16]{1,3,2,0:T(8,128)(4,1)S(1)} %copy.72), kind=kLoop, calls=%fused_computation.11 | loop fusion | flops 2096640 | bytes 2102272 | tf_op jit(solution)/shard_map/reduce_sum | solution.py:51
  24.7 0.1 reshape_reshape.11
  24.8 15.1 %all-gather.2 = f32[16,2,4,16]{3,2,1,0:T(4,128)S(1)} all-gather(f32[4,2,4,16]{3,2,1,0:T(4,128)S(1)} %copy.88), channel_id=4, replica_groups=mesh['groups'=2,'ctx'=4,'peer'=4] {'ctx'}, dimensions={0}, use_global_device_ids=true | all-gather | bytes 10240 | tf_op jit(solution)/shard_map/all_gather | solution.py:74
  40.0 13.6 %all-gather = f32[16,2,4,16]{3,2,1,0:T(4,128)S(1)} all-gather(f32[4,2,4,16]{3,2,1,0:T(4,128)S(1)} %copy.76), channel_id=2, replica_groups=mesh['groups'=2,'ctx'=4,'peer'=4] {'ctx'}, dimensions={0}, use_global_device_ids=true | all-gather | bytes 10240 | tf_op jit(solution)/shard_map/all_gather | solution.py:73
  53.7 0.6 copy.78
  54.3 3.2 %all-to-all-start = ((f32[1,2,4,16]{3,1,0,2:T(2,128)}), f32[1,2,4,16]{3,1,0,2:T(2,128)S(1)}, u32[]{:S(2)}, u32[]{:S(2)}) async-start(f32[1,2,4,16]{3,1,0,2:T(2,128)} %copy.78), calls=%async_computation | async-start | bytes 8192 | tf_op jit(solution)/shard_map/all_to_all | solution.py:82
  57.5 0.6 copy.91
  58.1 3.2 %all-to-all-done = f32[1,2,4,16]{3,1,0,2:T(2,128)S(1)} async-done(((f32[1,2,4,16]{3,1,0,2:T(2,128)}), f32[1,2,4,16]{3,1,0,2:T(2,128)S(1)}, u32[]{:S(2)}, u32[]{:S(2)}) %all-to-all-start) | async-done | bytes 544 | tf_op jit(solution)/shard_map/all_to_all | solution.py:82
  61.3 3.2 %all-to-all-start.2 = ((f32[1,2,4,16]{3,1,0,2:T(2,128)}), f32[1,2,4,16]{3,1,0,2:T(2,128)S(1)}, u32[]{:S(2)}, u32[]{:S(2)}) async-start(f32[1,2,4,16]{3,1,0,2:T(2,128)} %copy.91), calls=%async_computation.2 | async-start | bytes 8192 | tf_op jit(solution)/shard_map/all_to_all | solution.py:83
  64.5 3.7 %all-to-all-done.2 = f32[1,2,4,16]{3,1,0,2:T(2,128)S(1)} async-done(((f32[1,2,4,16]{3,1,0,2:T(2,128)}), f32[1,2,4,16]{3,1,0,2:T(2,128)S(1)}, u32[]{:S(2)}, u32[]{:S(2)}) %all-to-all-start.2) | async-done | bytes 544 | tf_op jit(solution)/shard_map/all_to_all | solution.py:83
  68.3 0.0 all-gather.5.cloned.1.call-done
  68.3 1.4 copy.84
  69.7 0.1 fusion.20
  69.8 0.1 bitcast_multiply_fusion.2
  69.9 0.6 copy.85
  70.5 3.3 %all-to-all-start.1 = ((f32[1,2,4,16,128]{4,3,1,0,2:T(8,128)}), f32[1,2,4,16,128]{4,3,1,0,2:T(8,128)S(1)}, u32[]{:S(2)}, u32[]{:S(2)}) async-start(f32[1,2,4,16,128]{4,3,1,0,2:T(8,128)} %copy.85), calls=%async_computation.1 | async-start | bytes 131072 | tf_op jit(solution)/shard_map/all_to_all | solution.py:81
  73.8 0.0 reduce-scatter.4.cloned.1.call-start
  73.9 4.0 %all-to-all-done.1 = f32[1,2,4,16,128]{4,3,1,0,2:T(8,128)S(1)} async-done(((f32[1,2,4,16,128]{4,3,1,0,2:T(8,128)}), f32[1,2,4,16,128]{4,3,1,0,2:T(8,128)S(1)}, u32[]{:S(2)}, u32[]{:S(2)}) %all-to-all-start.1) | async-done | bytes 65568 | tf_op jit(solution)/shard_map/all_to_all | solution.py:81
  77.9 0.1 fusion.22
  78.0 0.1 fusion.27
  78.1 12.8 %convolution_bitcast_fusion = f32[8192,2]{0,1:T(2,128)S(1)} fusion(bf16[2048,8192]{1,0:T(8,128)(2,1)} %param.9, bf16[1,2,16,128]{3,2,1,0:T(8,128)(2,1)S(1)} %fusion.27), kind=kOutput, calls=%fused_computation | convolution fusion | flops 67108864 | bytes 33628160 | tf_op jit(solution)/shard_map/dot_general | solution.py:89
  90.9 2.6 %copy.105 = f32[8192,2]{1,0:T(8,128)} copy(f32[8192,2]{0,1:T(2,128)S(1)} %convolution_bitcast_fusion) | data formatting | bytes 131072
  93.5 0.0 reduce-scatter.4.cloned.1.call-update
  93.6 77.1 %reduce-scatter.4.cloned.1.call-done = f32[2048,2]{1,0:T(8,128)} async-done(((f32[8192,2]{1,0:T(8,128)}), f32[2048,2]{1,0:T(8,128)}) %reduce-scatter.4.cloned.1.call-update) | async-done | bytes 16400
  170.7 1.6 copy.106
  172.2 0.6 copy.94
  (16 shorter events, 0.2 us)
Async XLA Ops:
  6.5 2.2 %copy-start = (bf16[2,4,64,128]{3,2,1,0:T(8,128)(2,1)S(1)}, bf16[2,4,64,128]{3,2,1,0:T(8,128)(2,1)}, u32[]{:S(2)}) copy-start(bf16[2,4,64,128]{3,2,1,0:T(8,128)(2,1)} %param.5) | copy-start | bytes 393220
  6.5 61.8 %all-gather.5.cloned.1.call-start = ((), (), s32[]{:S(2)}) async-start(), calls=%async_computation.4 | async-start | bytes 1310720 | tf_op jit(solution)/shard_map/all_gather | solution.py:72
  8.8 6.1 %copy-start.2 = (bf16[2,16,8,64,128]{4,3,2,1,0:T(8,128)(2,1)S(1)}, bf16[2,16,8,64,128]{4,3,2,1,0:T(8,128)(2,1)}, u32[]{:S(2)}) copy-start(bf16[2,16,8,64,128]{4,3,2,1,0:T(8,128)(2,1)} %param.7) | copy-start | bytes 12582916
  14.9 5.0 %copy-start.1 = (f32[2,8,16,64,4,8]{3,5,4,2,1,0:T(8,128)}, f32[2,8,16,64,4,8]{3,5,4,2,1,0:T(8,128)S(1)}, u32[]{:S(2)}) copy-start(f32[2,8,16,64,4,8]{3,5,4,2,1,0:T(8,128)S(1)} %get-tuple-element.10) | copy-start | bytes 6291460
  54.3 7.0 %all-to-all-start = ((f32[1,2,4,16]{3,1,0,2:T(2,128)}), f32[1,2,4,16]{3,1,0,2:T(2,128)S(1)}, u32[]{:S(2)}, u32[]{:S(2)}) async-start(f32[1,2,4,16]{3,1,0,2:T(2,128)} %copy.78), calls=%async_computation | async-start | bytes 8192 | tf_op jit(solution)/shard_map/all_to_all | solution.py:82
  61.3 7.0 %all-to-all-start.2 = ((f32[1,2,4,16]{3,1,0,2:T(2,128)}), f32[1,2,4,16]{3,1,0,2:T(2,128)S(1)}, u32[]{:S(2)}, u32[]{:S(2)}) async-start(f32[1,2,4,16]{3,1,0,2:T(2,128)} %copy.91), calls=%async_computation.2 | async-start | bytes 8192 | tf_op jit(solution)/shard_map/all_to_all | solution.py:83
  70.5 7.4 %all-to-all-start.1 = ((f32[1,2,4,16,128]{4,3,1,0,2:T(8,128)}), f32[1,2,4,16,128]{4,3,1,0,2:T(8,128)S(1)}, u32[]{:S(2)}, u32[]{:S(2)}) async-start(f32[1,2,4,16,128]{4,3,1,0,2:T(8,128)} %copy.85), calls=%async_computation.1 | async-start | bytes 131072 | tf_op jit(solution)/shard_map/all_to_all | solution.py:81
  73.8 96.8 %reduce-scatter.4.cloned.1.call-start = ((), (), s32[]{:S(2)}) async-start(), calls=%async_computation.5 | async-start | bytes 5242880
Sparse Core Ops, SparseCore 0:
  20.8 31.9 all-gather.4
  93.7 76.9 reduce-scatter.3
where the time goes:
time: 180 us
  waiting for transfers between devices  88 us (49%)
  blocking collectives  28.8 us (16%)
  matrix products  23.9 us (13%)
  between operations  13.6 us (8%)
  starting transfers between devices  9.82 us (5%)
  local copies, waits for them, and re-layouts  9.13 us (5%)
  other arithmetic  6.45 us (4%)
    unnamed x3, waiting for transfers between devices  77.1 us
    all_gather x1, blocking collectives, body(): lax.all_gather(blocks[2], 'ctx', axis=0, tiled=True)  15.1 us
    all_gather x1, blocking collectives, body(): lax.all_gather(blocks[1], 'ctx', axis=0, tiled=True)  13.6 us
    dot_general x1, matrix products, body(): lax.dot_general(out_weight, attended, (((0,), (1,)), ((), ())), preferred...  12.8 us
    dot_general x1, matrix products, body(): jnp.einsum('bshgd,bphtd->bshgpt', grouped, key_cache, preferred_element_t...  6.09 us
    dot_general x1, matrix products, body(): jnp.einsum('bshgpt,bphtd->bshgd', weights.astype(jnp.bfloat16), value_cac...  4.98 us
    unnamed x8, local copies, waits for them, and re-layouts  4.17 us
    all_to_all x1, waiting for transfers between devices, body(): lax.all_to_all(ctx_part[0][None], 'peer', split_axis=2, concat_axis=0, ti...  4.01 us
  transfers between devices with their start and end apart: 5, of which 4 were waited for; matrix products, arithmetic and copies ran while one was open for 3% of the time, Pallas kernels for 0%

commit v1 on v0

v1 whole, which is shorter than its diff:
```python
import functools
import math

import jax
import jax.numpy as jnp
from jax import lax
from jax.experimental import pallas as pl
from jax.experimental.pallas import tpu as pltpu
from jax.sharding import PartitionSpec as P

masked_score = -1e30
least_maximum = -1e20
LANES = 128
HALF = LANES // 2


def kernel(
    dims,
    q_ref, list_ref, key_ref, value_ref, weight_ref, out_ref,
    kbuf, vbuf, wbuf, qs, mask, send_a, recv_a, send_b, recv_b, gat, send_c, recv_c,
    k_sem, v_sem, w_sem, sa_sem, ra_sem, sb_sem, rb_sem, sg_sem, rg_sem, sc_sem, rc_sem,
):
    C, N, B, S, KV, G, HD, PG, PAGE, D = dims
    SS = S // N
    KC = max(1, KV // C)
    NB = KV // KC
    R = C // NB
    HS = KV * G // C
    Q = C // N
    U = SS * B * KC
    rows = U * G
    tokens = PG * PAGE
    scale = HD ** (-0.5) * math.log2(math.e)
    c = lax.axis_index("ctx")
    p = lax.axis_index("peer")
    own = c // R
    place = lax.rem(c, R)

    def block_of(i):
        return lax.rem(own + 1 + i, NB)

    loads = []
    for i in range(NB):
        heads = pl.ds(block_of(i) * KC, KC)
        loads.append((
            pltpu.make_async_copy(key_ref.at[:, :, heads], kbuf.at[i], k_sem.at[i]),
            pltpu.make_async_copy(value_ref.at[:, :, heads], vbuf.at[i], v_sem.at[i]),
        ))
    for pair in loads:
        pair[0].start()
        pair[1].start()
    columns = pl.ds(pl.multiple_of(p * (D // N), LANES), D // N)
    w_load = pltpu.make_async_copy(weight_ref.at[:, columns], wbuf, w_sem)
    w_load.start()

    barrier = pltpu.get_barrier_semaphore()
    for dc in range(C):
        for dp in range(N):
            if dc or dp:
                pl.semaphore_signal(
                    barrier, inc=1,
                    device_id={"ctx": lax.rem(c + dc, C), "peer": lax.rem(p + dp, N)},
                    device_id_type=pl.DeviceIdType.MESH,
                )

    for b in range(B):
        for s in range(S):
            some = q_ref[b, s].astype(jnp.float32)
            for h in range(KV):
                qs[h, b, s * G:(s + 1) * G, :] = some[h * G:(h + 1) * G]
    first = (c * N + p) * PG
    ids = list_ref[...].reshape(B * S * KV, list_ref.shape[3])
    per_tile = LANES // PAGE
    lane_page = lax.broadcasted_iota(jnp.int32, (ids.shape[1], LANES), 1) // PAGE
    for j in range(tokens // LANES):
        listed = jnp.zeros((B * S * KV, LANES), jnp.float32)
        for k in range(per_tile):
            equal = jnp.where(ids == first + (j * per_tile + k), 1.0, 0.0).astype(jnp.bfloat16)
            spread = jnp.where(lane_page == k, 1.0, 0.0).astype(jnp.bfloat16)
            listed += jnp.dot(equal, spread, preferred_element_type=jnp.float32)
        mask[:, j * LANES:(j + 1) * LANES] = listed

    lane = lax.broadcasted_iota(jnp.int32, (G, LANES), 1)

    def attend(i):
        blk = block_of(i)
        tiles = [jnp.zeros((G, LANES), jnp.float32)] * N
        loads[i][0].wait()
        loads[i][1].wait()
        for b in range(B):
            for kc in range(KC):
                h = blk * KC + kc
                q = qs[h, b].astype(jnp.bfloat16)
                keys = kbuf[i, b, :, kc].reshape(tokens, HD)
                values = vbuf[i, b, :, kc].reshape(tokens, HD)
                score = lax.dot_general(
                    q, keys, (((1,), (1,)), ((), ())), preferred_element_type=jnp.float32
                )
                listed = jnp.concatenate([
                    jnp.broadcast_to(mask[pl.ds((b * S + s) * KV + h, 1), :], (G, tokens))
                    for s in range(S)
                ], axis=0)
                score = jnp.where(listed > 0.5, score * scale, masked_score)
                top = jnp.maximum(jnp.max(score, axis=1, keepdims=True), least_maximum)
                weights = jnp.exp2(score - top)
                total = jnp.sum(weights, axis=1, keepdims=True)
                blended = jnp.dot(
                    weights.astype(jnp.bfloat16), values, preferred_element_type=jnp.float32
                )
                for s in range(S):
                    n, ss = divmod(s, SS)
                    u = (ss * B + b) * KC + kc
                    part = slice(s * G, (s + 1) * G)
                    send_a[i, n, u * G:(u + 1) * G, :] = blended[part]
                    tiles[n] = jnp.where(
                        lane == u, top[part], jnp.where(lane == HALF + u, total[part], tiles[n])
                    )
        for n in range(N):
            send_a[i, n, rows:rows + G, :] = tiles[n]

    def copies_a(i):
        made = []
        for d in range(1, N):
            to = lax.rem(p + d, N)
            made.append(pltpu.make_async_remote_copy(
                src_ref=send_a.at[i, to], dst_ref=recv_a.at[i, d - 1],
                send_sem=sa_sem.at[i, d - 1], recv_sem=ra_sem.at[i, d - 1],
                device_id={"peer": to}, device_id_type=pl.DeviceIdType.MESH,
            ))
        return made

    def copies_b(i):
        made = []
        for dr in range(R):
            if i == NB - 1 and dr == 0:
                continue
            slot = i * R + dr - (1 if i == NB - 1 else 0)
            to = block_of(i) * R + lax.rem(place + dr, R)
            made.append(pltpu.make_async_remote_copy(
                src_ref=send_b.at[i], dst_ref=recv_b.at[slot],
                send_sem=sb_sem.at[slot], recv_sem=rb_sem.at[slot],
                device_id={"ctx": to}, device_id_type=pl.DeviceIdType.MESH,
            ))
        return made

    def factors(tiles):
        top = functools.reduce(jnp.maximum, tiles)
        scales = [jnp.exp2(t - top) for t in tiles]
        total = sum(f * pltpu.roll(t, HALF, 1) for f, t in zip(scales, tiles))
        return top, scales, total

    def blend(parts, scales, u):
        return sum(
            part[u * G:(u + 1) * G, :] * f[:, u:u + 1] for part, f in zip(parts, scales)
        )

    def fold_a(i):
        parts = [send_a.at[i, p]] + [recv_a.at[i, d] for d in range(N - 1)]
        tiles = [part[rows:rows + G, :] for part in parts]
        top, scales, total = factors(tiles)
        for u in range(U):
            send_b[i, u * G:(u + 1) * G, :] = blend(parts, scales, u)
        send_b[i, rows:rows + G, :] = jnp.where(lane < HALF, top, pltpu.roll(total, HALF, 1))

    all_a, all_b = [], []
    for i in range(NB + 1):
        if i < NB:
            attend(i)
            if i == 0:
                pl.semaphore_wait(barrier, C * N - 1)
            all_a.append(copies_a(i))
            for copy in all_a[i]:
                copy.start()
        if i > 0:
            for copy in all_a[i - 1]:
                copy.wait_recv()
            fold_a(i - 1)
            made = copies_b(i - 1)
            for copy in made:
                copy.start()
            all_b += made

    for copy in all_b:
        copy.wait_recv()
    parts = [send_b.at[NB - 1]] + [recv_b.at[d] for d in range(C - 1)]
    top, scales, total = factors([part[rows:rows + G, :] for part in parts])
    scales = [f / total for f in scales]
    mine = pl.ds(pl.multiple_of(p * rows, 8), rows)
    attended = jnp.concatenate([blend(parts, scales, u) for u in range(U)], axis=0)
    gat[mine, :] = attended
    all_g = []
    for d in range(1, N):
        to = lax.rem(p + d, N)
        all_g.append(pltpu.make_async_remote_copy(
            src_ref=gat.at[mine], dst_ref=gat.at[mine],
            send_sem=sg_sem.at[d - 1], recv_sem=rg_sem.at[d - 1],
            device_id={"peer": to}, device_id_type=pl.DeviceIdType.MESH,
        ))
    for copy in all_g:
        copy.start()
    w_load.wait()
    for d in range(1, N):
        theirs = gat.at[pl.ds(pl.multiple_of(lax.rem(p + N - d, N) * rows, 8), rows)]
        pltpu.make_async_remote_copy(
            src_ref=theirs, dst_ref=theirs,
            send_sem=sg_sem.at[d - 1], recv_sem=rg_sem.at[d - 1],
            device_id={"peer": lax.rem(p + d, N)}, device_id_type=pl.DeviceIdType.MESH,
        ).wait_recv()

    left = jnp.concatenate([
        gat[pl.ds((place * HS if R > 1 else 0) + j, S * B, stride=KC * G), :] for j in range(HS)
    ], axis=1).astype(jnp.bfloat16)
    product = jnp.dot(left, wbuf[...], preferred_element_type=jnp.float32)
    width = D // C
    for q in range(Q):
        for n in range(N):
            send_c[q, n] = product[n * SS * B:(n + 1) * SS * B, q * width:(q + 1) * width]

    def copy_c(q, dn):
        to = lax.rem(p + dn, N)
        return pltpu.make_async_remote_copy(
            src_ref=send_c.at[q, to], dst_ref=recv_c.at[c],
            send_sem=sc_sem.at[q, dn], recv_sem=rc_sem.at[c],
            device_id={"ctx": p * Q + q, "peer": to}, device_id_type=pl.DeviceIdType.MESH,
        )

    for q in range(Q):
        for dn in range(1, N):
            copy_c(q, dn).start()

        @pl.when(p * Q + q != c)
        def _():
            copy_c(q, 0).start()

        @pl.when(p * Q + q == c)
        def _():
            recv_c[c] = send_c[q, p]

    def wait_c(source):
        pltpu.make_async_remote_copy(
            src_ref=send_c.at[0, 0], dst_ref=recv_c.at[source],
            send_sem=sc_sem.at[0, 0], recv_sem=rc_sem.at[source],
            device_id={"ctx": source, "peer": c // Q}, device_id_type=pl.DeviceIdType.MESH,
        ).wait_recv()

    for dc in range(1, C):
        wait_c(lax.rem(c + dc, C))

    @pl.when(p != c // Q)
    def _():
        wait_c(c)

    out_ref[...] = functools.reduce(jnp.add, [recv_c[k] for k in range(C)])

    for copies in all_a:
        for copy in copies:
            copy.wait_send()
    for copy in all_b + all_g:
        copy.wait_send()
    for q in range(Q):
        for dn in range(1, N):
            copy_c(q, dn).wait_send()

        @pl.when(p * Q + q != c)
        def _():
            copy_c(q, 0).wait_send()


def body(queries, key_cache, value_cache, page_list, out_weight):
    B, S, HQ, HD = queries.shape
    PG, KV, PAGE = key_cache.shape[1:4]
    D = out_weight.shape[1]
    C = lax.axis_size("ctx")
    N = lax.axis_size("peer")
    G = HQ // KV
    SS = S // N
    KC = max(1, KV // C)
    NB = KV // KC
    Q = C // N
    rows = SS * B * KC * G
    f32, bf16 = jnp.float32, jnp.bfloat16
    dma = pltpu.SemaphoreType.DMA
    dims = (C, N, B, S, KV, G, HD, PG, PAGE, D)
    vmem = pl.BlockSpec(memory_space=pltpu.VMEM)
    hbm = pl.BlockSpec(memory_space=pl.ANY)
    out = pl.pallas_call(
        functools.partial(kernel, dims),
        out_shape=jax.ShapeDtypeStruct((SS * B, D // C), f32),
        in_specs=[vmem, vmem, hbm, hbm, hbm],
        out_specs=vmem,
        scratch_shapes=[
            pltpu.VMEM((NB, B, PG, KC, PAGE, HD), bf16),
            pltpu.VMEM((NB, B, PG, KC, PAGE, HD), bf16),
            pltpu.VMEM((out_weight.shape[0], D // N), bf16),
            pltpu.VMEM((KV, B, S * G, HD), f32),
            pltpu.VMEM((B * S * KV, PG * PAGE), f32),
            pltpu.VMEM((NB, N, rows + G, HD), f32),
            pltpu.VMEM((NB, N - 1, rows + G, HD), f32),
            pltpu.VMEM((NB, rows + G, HD), f32),
            pltpu.VMEM((C - 1, rows + G, HD), f32),
            pltpu.VMEM((N * rows, HD), f32),
            pltpu.VMEM((Q, N, SS * B, D // C), f32),
            pltpu.VMEM((C, SS * B, D // C), f32),
            dma((NB,)), dma((NB,)), dma,
            dma((NB, N - 1)), dma((NB, N - 1)),
            dma((C - 1,)), dma((C - 1,)),
            dma((N - 1,)), dma((N - 1,)),
            dma((Q, N)), dma((C,)),
        ],
        compiler_params=pltpu.CompilerParams(
            collective_id=0, has_side_effects=True, vmem_limit_bytes=48 * 2**20
        ),
        name="paged_attention_projection",
    )(queries, page_list, key_cache, value_cache, out_weight)
    return out.reshape(SS, B, D // C).swapaxes(0, 1)


def solution(mesh):
    in_specs = (
        P("groups", None, None, None),
        P("groups", ("ctx", "peer"), None, None, None),
        P("groups", ("ctx", "peer"), None, None, None),
        P("groups", None, None, None),
        P("ctx", None),
    )
    out_specs = P("groups", "peer", "ctx")
    return jax.shard_map(body, mesh=mesh, in_specs=in_specs, out_specs=out_specs, check_vma=False)
```

time: 180 us -> 30.9 us (0.17)
  waiting for transfers between devices: 88 us -> 0 us
  blocking collectives: 28.8 us -> 0 us
  Pallas kernels: 0 us -> 26.2 us
  matrix products: 23.9 us -> 0 us
  between operations: 13.6 us -> 0.01 us
  starting transfers between devices: 9.82 us -> 0 us
  other arithmetic: 6.45 us -> 0 us
  local copies, waits for them, and re-layouts: 9.13 us -> 4.47 us
    unnamed x3 -> x0, waiting for transfers between devices: 77.1 us -> none
    all_gather x2 -> x0, blocking collectives: 28.8 us -> none  [the longest x1 15.1 us: body(): lax.all_gather(blocks[2], 'ctx', axis=0, tiled=True)]
    pallas_call x0 -> x1, Pallas kernels: none -> 26.2 us  [body(): pl.pallas_call(functools.partial(kernel, dims), out_shape=jax.ShapeDtypeS...]
    dot_general x3 -> x0, matrix products: 23.9 us -> none  [the longest x1 12.8 us: body(): lax.dot_general(out_weight, attended, (((0,), (1,)), ((), ())), preferred...]
    all_to_all x3 -> x0, waiting for transfers between devices: 10.9 us -> none  [the longest x1 4.01 us: body(): lax.all_to_all(ctx_part[0][None], 'peer', split_axis=2, concat_axis=0, ti...]
    all_to_all x3 -> x0, starting transfers between devices: 9.77 us -> none  [the longest x1 3.28 us: body(): lax.all_to_all(ctx_part[0][None], 'peer', split_axis=2, concat_axis=0, ti...]
    reduce_sum x5 -> x0, other arithmetic: 4.2 us -> none  [the longest x1 3.94 us: body(): totals = jnp.sum(weights, axis=(4, 5))]
    reduce_or x1 -> x0, other arithmetic: 2.02 us -> none  [body(): chosen = jnp.any(page_list[..., None] == local_ids, axis=3)]
  transfers between devices with their start and end apart: 5 -> 0, of which waited for: 4 -> 0; matrix products, arithmetic and copies ran while one was open for 3% -> 0% of each run, Pallas kernels for 0% -> 0%
where the time goes in v1:
time: 30.9 us; the launch traced here: 30.7 us
  Pallas kernels  26.2 us (85%)
  local copies, waits for them, and re-layouts  4.47 us (14%)
    pallas_call x1, Pallas kernels, body(): pl.pallas_call(functools.partial(kernel, dims), out_shape=jax.ShapeDtypeS...  26.2 us
    unnamed x6, local copies, waits for them, and re-layouts  3.85 us
    another operation x1, local copies, waits for them, and re-layouts, body(): return out.reshape(SS, B, D // C).swapaxes(0, 1)  0.62 us

profile of v1, /device:TPU:0, one launch (start us, length us, event | category | flops | bytes accessed | tf_op | source)
XLA Modules:
  0.0 30.7 jit_solution(11127025257335539586)
XLA Ops:
  0.0 0.0 copy-start
  0.0 2.2 %copy-done = bf16[2,16,8,64,128]{4,3,2,1,0:T(8,128)(2,1)S(1)} copy-done((bf16[2,16,8,64,128]{4,3,2,1,0:T(8,128)(2,1)S(1)}, bf16[2,16,8,64,128]{4,3,2,1,0:T(8,128)(2,1)}, u32[]{:S(2)}) %copy-start) | copy-done | bytes 4194328
  2.2 0.0 copy-start.1
  2.2 0.9 %copy-done.1 = bf16[2,4,64,128]{3,2,1,0:T(8,128)(2,1)S(1)} copy-done((bf16[2,4,64,128]{3,2,1,0:T(8,128)(2,1)S(1)}, bf16[2,4,64,128]{3,2,1,0:T(8,128)(2,1)}, u32[]{:S(2)}) %copy-start.1) | copy-done | bytes 131096
  3.1 0.0 copy-start.2
  3.1 0.8 %copy-done.2 = s32[2,4,8,64]{3,2,1,0:T(8,128)S(1)} copy-done((s32[2,4,8,64]{3,2,1,0:T(8,128)S(1)}, s32[2,4,8,64]{3,2,1,0:T(8,128)}, u32[]{:S(2)}) %copy-start.2) | copy-done | bytes 16408
  3.9 26.2 %paged_attention_projection.1 = f32[2,2048]{1,0:T(2,128)S(1)} custom-call(bf16[2,4,64,128]{3,2,1,0:T(8,128)(2,1)S(1)} %copy-done.1, s32[2,4,8,64]{3,2,1,0:T(8,128)S(1)} %copy-done.2, bf16[2,16,8,64,128]{4,3,2,1,0:T(8,128)(2,1)S(1)} %copy-done, bf16[2,16,8,64,128]{4,3,2,1,0:T(8,128)(2,1)} %value_ref.1, bf16[2048,8192]{1,0:T(8,128)(2,1)} %weight_ref.1), custom_call_target="tpu_custom_call" | custom-call | tf_op jit(solution)/shard_map/paged_attention_projection/pallas_call | solution.py:286
  30.0 0.6 %copy.6 = f32[2,1,2048]{2,1,0:T(1,128)} copy(f32[2,1,2048]{2,0,1:T(2,128)S(1)} %bitcast.1) | data formatting | bytes 32768 | tf_op jit(solution)/shard_map/transpose;reshape | solution.py:315
Async XLA Ops:
  0.0 2.2 %copy-start = (bf16[2,16,8,64,128]{4,3,2,1,0:T(8,128)(2,1)S(1)}, bf16[2,16,8,64,128]{4,3,2,1,0:T(8,128)(2,1)}, u32[]{:S(2)}) copy-start(bf16[2,16,8,64,128]{4,3,2,1,0:T(8,128)(2,1)} %key_ref.1) | copy-start | bytes 12582916
  2.2 0.9 %copy-start.1 = (bf16[2,4,64,128]{3,2,1,0:T(8,128)(2,1)S(1)}, bf16[2,4,64,128]{3,2,1,0:T(8,128)(2,1)}, u32[]{:S(2)}) copy-start(bf16[2,4,64,128]{3,2,1,0:T(8,128)(2,1)} %q_ref.1) | copy-start | bytes 393220
  3.1 0.8 %copy-start.2 = (s32[2,4,8,64]{3,2,1,0:T(8,128)S(1)}, s32[2,4,8,64]{3,2,1,0:T(8,128)}, u32[]{:S(2)}) copy-start(s32[2,4,8,64]{3,2,1,0:T(8,128)} %list_ref.1) | copy-start | bytes 49156

commit v2 on v1

--- a/solution.py
+++ b/solution.py
@@ -26,7 +26,6 @@
     NB = KV // KC
     R = C // NB
     HS = KV * G // C
-    Q = C // N
     U = SS * B * KC
     rows = U * G
     tokens = PG * PAGE
@@ -49,9 +48,18 @@
     for pair in loads:
         pair[0].start()
         pair[1].start()
-    columns = pl.ds(pl.multiple_of(p * (D // N), LANES), D // N)
-    w_load = pltpu.make_async_copy(weight_ref.at[:, columns], wbuf, w_sem)
-    w_load.start()
+    width = D // C
+    sub = width // N
+    fine = sub % LANES == 0
+    w_loads = []
+    for k in range(C if fine else 1):
+        start, size = (k * width + p * sub, sub) if fine else (p * (D // N), D // N)
+        w_loads.append(pltpu.make_async_copy(
+            weight_ref.at[:, pl.ds(pl.multiple_of(start, LANES), size)],
+            wbuf.at[:, k * size:(k + 1) * size], w_sem.at[k],
+        ))
+    for load in w_loads:
+        load.start()
 
     barrier = pltpu.get_barrier_semaphore()
     for dc in range(C):
@@ -198,7 +206,8 @@
         ))
     for copy in all_g:
         copy.start()
-    w_load.wait()
+    for load in w_loads:
+        load.wait()
     for d in range(1, N):
         theirs = gat.at[pl.ds(pl.multiple_of(lax.rem(p + N - d, N) * rows, 8), rows)]
         pltpu.make_async_remote_copy(
@@ -211,10 +220,58 @@
         gat[pl.ds((place * HS if R > 1 else 0) + j, S * B, stride=KC * G), :] for j in range(HS)
     ], axis=1).astype(jnp.bfloat16)
     product = jnp.dot(left, wbuf[...], preferred_element_type=jnp.float32)
-    width = D // C
+    if fine:
+        spread_fine(C, N, SS * B, sub, product, out_ref, send_c, recv_c, sc_sem, rc_sem)
+    else:
+        spread_coarse(C, N, SS * B, width, product, out_ref, send_c, recv_c, sc_sem, rc_sem)
+
+    for copies in all_a:
+        for copy in copies:
+            copy.wait_send()
+    for copy in all_b + all_g:
+        copy.wait_send()
+
+
+def spread_fine(C, N, count, sub, product, out_ref, send_c, recv_c, sc_sem, rc_sem):
+    c = lax.axis_index("ctx")
+    p = lax.axis_index("peer")
+    for k in range(C):
+        for n in range(N):
+            send_c[k, n] = product[n * count:(n + 1) * count, k * sub:(k + 1) * sub]
+    others = [(dc, dn) for dc in range(C) for dn in range(N) if dc or dn]
+    copies = []
+    for dc, dn in others:
+        to_c, to_p = lax.rem(c + dc, C), lax.rem(p + dn, N)
+        copies.append(pltpu.make_async_remote_copy(
+            src_ref=send_c.at[to_c, to_p], dst_ref=recv_c.at[c, p],
+            send_sem=sc_sem.at[dc, dn], recv_sem=rc_sem.at[dc, dn],
+            device_id={"ctx": to_c, "peer": to_p}, device_id_type=pl.DeviceIdType.MESH,
+        ))
+    for copy in copies:
+        copy.start()
+    recv_c[c, p] = send_c[c, p]
+    for (dc, dn) in others:
+        from_c, from_p = lax.rem(c + C - dc, C), lax.rem(p + N - dn, N)
+        pltpu.make_async_remote_copy(
+            src_ref=send_c.at[from_c, from_p], dst_ref=recv_c.at[from_c, from_p],
+            send_sem=sc_sem.at[dc, dn], recv_sem=rc_sem.at[dc, dn],
+            device_id={"ctx": from_c, "peer": from_p}, device_id_type=pl.DeviceIdType.MESH,
+        ).wait_recv()
+    for n in range(N):
+        out_ref[:, n * sub:(n + 1) * sub] = functools.reduce(
+            jnp.add, [recv_c[k, n] for k in range(C)]
+        )
+    for copy in copies:
+        copy.wait_send()
+
+
+def spread_coarse(C, N, count, width, product, out_ref, send_c, recv_c, sc_sem, rc_sem):
+    c = lax.axis_index("ctx")
+    p = lax.axis_index("peer")
+    Q = C // N
     for q in range(Q):
         for n in range(N):
-            send_c[q, n] = product[n * SS * B:(n + 1) * SS * B, q * width:(q + 1) * width]
+            send_c[q, n] = product[n * count:(n + 1) * count, q * width:(q + 1) * width]
 
     def copy_c(q, dn):
         to = lax.rem(p + dn, N)
@@ -252,11 +309,6 @@
 
     out_ref[...] = functools.reduce(jnp.add, [recv_c[k] for k in range(C)])
 
-    for copies in all_a:
-        for copy in copies:
-            copy.wait_send()
-    for copy in all_b + all_g:
-        copy.wait_send()
     for q in range(Q):
         for dn in range(1, N):
             copy_c(q, dn).wait_send()
@@ -277,6 +329,8 @@
     KC = max(1, KV // C)
     NB = KV // KC
     Q = C // N
+    sub = D // C // N
+    fine = sub % LANES == 0
     rows = SS * B * KC * G
     f32, bf16 = jnp.float32, jnp.bfloat16
     dma = pltpu.SemaphoreType.DMA
@@ -299,16 +353,16 @@
             pltpu.VMEM((NB, rows + G, HD), f32),
             pltpu.VMEM((C - 1, rows + G, HD), f32),
             pltpu.VMEM((N * rows, HD), f32),
-            pltpu.VMEM((Q, N, SS * B, D // C), f32),
-            pltpu.VMEM((C, SS * B, D // C), f32),
-            dma((NB,)), dma((NB,)), dma,
+            pltpu.VMEM((C, N, SS * B, sub) if fine else (Q, N, SS * B, D // C), f32),
+            pltpu.VMEM((C, N, SS * B, sub) if fine else (C, SS * B, D // C), f32),
+            dma((NB,)), dma((NB,)), dma((C,)),
             dma((NB, N - 1)), dma((NB, N - 1)),
             dma((C - 1,)), dma((C - 1,)),
             dma((N - 1,)), dma((N - 1,)),
-            dma((Q, N)), dma((C,)),
+            dma((C, N) if fine else (Q, N)), dma((C, N) if fine else (C,)),
         ],
         compiler_params=pltpu.CompilerParams(
-            collective_id=0, has_side_effects=True, vmem_limit_bytes=48 * 2**20
+            collective_id=0, has_side_effects=True, vmem_limit_bytes=63 * 2**20
         ),
         name="paged_attention_projection",
     )(queries, page_list, key_cache, value_cache, out_weight)

time: 30.9 us -> 28.9 us (0.935)
  local copies, waits for them, and re-layouts: 4.47 us -> 1.34 us
  Pallas kernels: 26.2 us -> 27.3 us
    unnamed x6 -> x0, local copies, waits for them, and re-layouts: 3.85 us -> none
    pallas_call x1, Pallas kernels: 26.2 us -> 27.3 us  [body(): pl.pallas_call(functools.partial(kernel, dims), out_shape=jax.ShapeDtypeS...]
    another operation x1, local copies, waits for them, and re-layouts: 0.62 us -> 1.34 us  [body(): return out.reshape(SS, B, D // C).swapaxes(0, 1)]
where the time goes in v2:
time: 28.9 us; the launch traced here: 28.6 us
  Pallas kernels  27.3 us (94%)
  local copies, waits for them, and re-layouts  1.34 us (5%)
    pallas_call x1, Pallas kernels, body(): pl.pallas_call(functools.partial(kernel, dims), out_shape=jax.ShapeDtypeS...  27.3 us
    another operation x1, local copies, waits for them, and re-layouts, body(): return out.reshape(SS, B, D // C).swapaxes(0, 1)  1.34 us

profile of v2, /device:TPU:0, one launch (start us, length us, event | category | flops | bytes accessed | tf_op | source)
XLA Modules:
  0.0 28.6 jit_solution(13290438912484215754)
XLA Ops:
  0.0 27.3 %paged_attention_projection.1 = f32[2,2048]{1,0:T(2,128)} custom-call(bf16[2,4,64,128]{3,2,1,0:T(8,128)(2,1)} %q_ref.1, s32[2,4,8,64]{3,2,1,0:T(8,128)} %list_ref.1, bf16[2,16,8,64,128]{4,3,2,1,0:T(8,128)(2,1)} %key_ref.1, bf16[2,16,8,64,128]{4,3,2,1,0:T(8,128)(2,1)} %value_ref.1, bf16[2048,8192]{1,0:T(8,128)(2,1)} %weight_ref.1), custom_call_target="tpu_custom_call" | custom-call | tf_op jit(solution)/shard_map/paged_attention_projection/pallas_call | solution.py:340
  27.3 1.3 %copy.6 = f32[2,1,2048]{2,1,0:T(1,128)} copy(f32[2,1,2048]{2,0,1:T(2,128)} %bitcast.1) | data formatting | bytes 32768 | tf_op jit(solution)/shard_map/transpose;reshape | solution.py:369

commit v3 on v2

--- a/solution.py
+++ b/solution.py
@@ -258,9 +258,10 @@
             device_id={"ctx": from_c, "peer": from_p}, device_id_type=pl.DeviceIdType.MESH,
         ).wait_recv()
     for n in range(N):
-        out_ref[:, n * sub:(n + 1) * sub] = functools.reduce(
-            jnp.add, [recv_c[k, n] for k in range(C)]
-        )
+        whole = functools.reduce(jnp.add, [recv_c[k, n] for k in range(C)])
+        B = out_ref.shape[0]
+        for r in range(count):
+            out_ref[r % B, r // B:r // B + 1, n * sub:(n + 1) * sub] = whole[r:r + 1]
     for copy in copies:
         copy.wait_send()
 
@@ -307,7 +308,10 @@
     def _():
         wait_c(c)
 
-    out_ref[...] = functools.reduce(jnp.add, [recv_c[k] for k in range(C)])
+    whole = functools.reduce(jnp.add, [recv_c[k] for k in range(C)])
+    B = out_ref.shape[0]
+    for r in range(count):
+        out_ref[r % B, r // B:r // B + 1, :] = whole[r:r + 1]
 
     for q in range(Q):
         for dn in range(1, N):
@@ -339,7 +343,7 @@
     hbm = pl.BlockSpec(memory_space=pl.ANY)
     out = pl.pallas_call(
         functools.partial(kernel, dims),
-        out_shape=jax.ShapeDtypeStruct((SS * B, D // C), f32),
+        out_shape=jax.ShapeDtypeStruct((B, SS, D // C), f32),
         in_specs=[vmem, vmem, hbm, hbm, hbm],
         out_specs=vmem,
         scratch_shapes=[
@@ -366,7 +370,7 @@
         ),
         name="paged_attention_projection",
     )(queries, page_list, key_cache, value_cache, out_weight)
-    return out.reshape(SS, B, D // C).swapaxes(0, 1)
+    return out
 
 
 def solution(mesh):

time: 28.9 us -> 28.9 us (level)
    another operation x1 -> x0, local copies, waits for them, and re-layouts: 1.34 us -> none  [body(): return out.reshape(SS, B, D // C).swapaxes(0, 1)]
    unnamed x0 -> x1, local copies, waits for them, and re-layouts: none -> 1.32 us
where the time goes in v3:
time: 28.9 us; the launch traced here: 28.6 us
  Pallas kernels  27.3 us (94%)
  local copies, waits for them, and re-layouts  1.32 us (5%)
    pallas_call x1, Pallas kernels, body(): pl.pallas_call(functools.partial(kernel, dims), out_shape=jax.ShapeDtypeS...  27.3 us
    unnamed x1, local copies, waits for them, and re-layouts  1.32 us

profile of v3, /device:TPU:0, one launch (start us, length us, event | category | flops | bytes accessed | tf_op | source)
XLA Modules:
  0.0 28.6 jit_solution(15088715884980607744)
XLA Ops:
  0.0 27.3 %paged_attention_projection.1 = f32[2,1,2048]{2,1,0:T(1,128)} custom-call(bf16[2,4,64,128]{3,2,1,0:T(8,128)(2,1)} %q_ref.1, s32[2,4,8,64]{3,2,1,0:T(8,128)} %list_ref.1, bf16[2,16,8,64,128]{4,3,2,1,0:T(8,128)(2,1)} %key_ref.1, bf16[2,16,8,64,128]{4,3,2,1,0:T(8,128)(2,1)} %value_ref.1, bf16[2048,8192]{1,0:T(8,128)(2,1)} %weight_ref.1), custom_call_target="tpu_custom_call" | custom-call | tf_op jit(solution)/shard_map/paged_attention_projection/pallas_call | solution.py:344
  27.3 1.3 %copy.7 = f32[2,1,2048]{2,1,0:T(1,128)} copy(f32[2,1,2048]{2,1,0:T(1,128)} %paged_attention_projection.1) | data formatting | bytes 32768
